TPU v7x, 32 devices: a whole 2x2x4 slice. The times are simulated.
32 devices in a mesh: groups: 2 (over x), blk: 16 (over z, y, core).
Axes of the slice: x: 2, y: 2, z: 4, core: 2. Of those that a mesh axis runs over, the one named last changes fastest.
Arguments:
- in_factors: bfloat16 [32768, 16, 64], P(('groups', 'blk')), parts along dimension 0, may hold values from -6 to 6
- out_factors: bfloat16 [32768, 16, 64], P(('groups', 'blk')), parts along dimension 0, may hold values from -6 to 6
- token_counts: int32 [32768], P(('groups', 'blk')), parts along dimension 0, may hold values from 1 to 16, as said below
- train_cluster: int32 [32768], P(('groups', 'blk')), parts along dimension 0, may hold values from 0 to 3
- queries: bfloat16 [4096, 4096], P(('groups', 'blk')), parts along dimension 0, may hold values from -6 to 6
- query_cluster: int32 [4096], P('groups'), parts along dimension 0, may hold values from 0 to 3
- pair_mask: int32 [256, 9], P(('groups', 'blk')), parts along dimension 0, may hold values from 0 to 1
Outputs:
- train_score: float32 [32768], P(('groups', 'blk')), parts along dimension 0
- query_score: float32 [4096], P(('groups', 'blk')), parts along dimension 0
There are 2 independent parts, one for each index of `groups`. A program takes and returns all parts, laid end to end along the dimension named above; each array names one. Nothing has to cross between parts.
Inputs may be any that keep to these rules, and one draw needn't show every extreme that they name: `token_counts`: each train row has at least one counted token, and some row reaches 16.
All inputs are finite; a program needn't handle non-finite values.
Results may differ from a plain program's by a relative error of at most 0.00046.
Values may be sent and summed in bfloat16 or wider, within the bound.
A program may use at most 128 MiB of HBM per device.

v0:
```python
import jax
import jax.numpy as jnp
from jax import lax
from jax.sharding import PartitionSpec as P


def passed_along(value, axis, by):
    devices = lax.axis_size(axis)
    return lax.ppermute(value, axis, [(i, (i + by) % devices) for i in range(devices)])


def per_device(
    in_factors, out_factors, token_counts, train_cluster, queries, query_cluster, pair_mask
):
    train_rows = in_factors.shape[0]
    slots = in_factors.shape[1]
    tile_rows = queries.shape[0]
    width = queries.shape[1]
    band = pair_mask.shape[1]
    reach = (band - 1) // 2
    inv = 1.0 / width**0.5
    nblocks = lax.axis_size("blk")
    index = lax.axis_index("blk")
    live = jnp.arange(slots, dtype=jnp.int32)[None, :] < token_counts[:, None]
    left = jnp.where(live[:, :, None], in_factors, jnp.zeros_like(in_factors))
    sketch = jnp.einsum("rti,rto->rio", left, out_factors, preferred_element_type=jnp.float32)
    sketch = sketch.reshape(train_rows, width).astype(jnp.bfloat16)
    clusters_all = query_cluster.reshape(nblocks, tile_rows)

    def score_block(visiting, offset):
        source = (index + offset) % nblocks
        qclus = lax.dynamic_index_in_dim(clusters_all, source, 0, keepdims=False)
        scores = jnp.dot(sketch, visiting.T, preferred_element_type=jnp.float32) * inv
        rowmask = jnp.repeat(pair_mask[:, offset + reach], tile_rows).astype(jnp.float32)
        weight = (train_cluster[:, None] == qclus[None, :]).astype(jnp.float32) * rowmask[:, None]
        weighted = weight * jnp.maximum(scores, 0.0)
        return (jnp.sum(weighted, axis=1), jnp.sum(weighted, axis=0))

    train_total, query_total = score_block(queries, 0)
    partials = []
    current = queries
    for step in range(reach):
        current = passed_along(current, "blk", -1)
        tpart, qpart = score_block(current, step + 1)
        train_total = train_total + tpart
        partials.append((qpart, step + 1))
    current = queries
    for step in range(reach):
        current = passed_along(current, "blk", 1)
        tpart, qpart = score_block(current, -(step + 1))
        train_total = train_total + tpart
        partials.append((qpart, -(step + 1)))
    for qpart, offset in partials:
        query_total = query_total + passed_along(qpart, "blk", offset)
    return (train_total / 32.0, query_total / 32.0)


def solution(mesh):
    placed = (
        P(("groups", "blk"), None, None),
        P(("groups", "blk"), None, None),
        P(("groups", "blk")),
        P(("groups", "blk")),
        P(("groups", "blk"), None),
        P("groups"),
        P(("groups", "blk"), None),
    )
    return jax.shard_map(
        per_device,
        mesh=mesh,
        in_specs=placed,
        out_specs=(P(("groups", "blk")), P(("groups", "blk"))),
        check_vma=False,
    )
```

profile of v0, /device:TPU:0, one launch (start us, length us, event | category | flops | bytes accessed | tf_op | source)
XLA Modules:
  0.0 146.7 jit_solution(17256412066846282327)
XLA Ops:
  1.1 5.1 %collective-permute-start = (bf16[128,4096]{1,0:T(8,128)(2,1)}, bf16[128,4096]{1,0:T(8,128)(2,1)S(1)}, u32[]{:S(2)}, u32[]{:S(2)}) collective-permute-start(bf16[128,4096]{1,0:T(8,128)(2,1)} %param.11), channel_id=1, source_target_pairs={{0,15},{1,0},{2,1},{3,2},{4,3},{5,4},{6,5},{7,6},{8,7},{9,8},{10,9... | collective-permute-start | bytes 3145736 | tf_op jit(solution)/shard_map/ppermute | solution.py:9
  6.9 1.8 %broadcast_select_fusion = bf16[1024,16,64]{0,2,1:T(8,128)(2,1)S(1)} fusion(bf16[1024,16,64]{0,2,1:T(8,128)(2,1)} %param.7, pred[1024,16]{0,1:T(8,128)(4,1)S(1)} %iota_compare_fusion), kind=kLoop, calls=%fused_computation.1 | loop fusion | flops 1048576 | bytes 4210688 | tf_op jit(solution)/shard_map/jit(_where)/select_n | solution.py:25
  8.7 4.9 %copy.11 = bf16[1024,16,64]{2,1,0:T(8,128)(2,1)} copy(bf16[1024,16,64]{0,2,1:T(8,128)(2,1)S(1)} %broadcast_select_fusion) | data formatting | bytes 4194304 | tf_op jit(solution)/shard_map/jit(_where)/select_n | solution.py:25
  13.6 6.2 %copy.12 = bf16[1024,16,64]{2,1,0:T(8,128)(2,1)} copy(bf16[1024,16,64]{0,2,1:T(8,128)(2,1)} %param.8) | data formatting | bytes 4194304 | tf_op args[1]
  19.8 10.6 %convolution_convert_fusion = bf16[1024,64,64]{2,1,0:T(8,128)(2,1)} fusion(bf16[1024,16,64]{2,1,0:T(8,128)(2,1)} %copy.11, bf16[1024,16,64]{2,1,0:T(8,128)(2,1)} %copy.12), kind=kOutput, calls=%fused_computation | convolution fusion | flops 138412032 | bytes 12582912 | tf_op jit(solution)/shard_map/rti,rto->rio/dot_general | solution.py:26
  30.3 18.4 %copy.13 = bf16[1024,64,64]{0,2,1:T(8,128)(2,1)} copy(bf16[1024,64,64]{2,1,0:T(8,128)(2,1)} %convolution_convert_fusion) | data formatting | bytes 16777216 | tf_op jit(solution)/shard_map/convert_element_type | solution.py:27
  49.7 6.2 %fusion.28 = (f32[128]{0:T(128)S(1)}, f32[1024]{0:T(1024)S(1)}) fusion(bf16[1024,4096]{0,1:T(8,128)(2,1)} %bitcast.58, bf16[128,4096]{1,0:T(8,128)(2,1)S(1)} %copy-done.3, f32[1024]{0:T(1024)S(1)} %broadcast_bitcast_fusion.8, s32[128]{0:T(128)S(1)} %get-tuple-element.37, s32[1024]{0:T(1024)S(1)} %copy-done.4), kind=kOutput, calls=%fused_computation.69 | convolution fusion | flops 1074658176 | bytes 9450496 | tf_op jit(solution)/shard_map/dot_general | solution.py:33
  56.1 4.4 %collective-permute-start.1 = (bf16[128,4096]{1,0:T(8,128)(2,1)S(1)}, bf16[128,4096]{1,0:T(8,128)(2,1)S(1)}, u32[]{:S(2)}, u32[]{:S(2)}) collective-permute-start(bf16[128,4096]{1,0:T(8,128)(2,1)S(1)} %collective-permute-done), channel_id=1, source_target_pairs={{0,15},{1,0},{2,1},{3,2},{4,3},{5,4},{6,5},{7,6},{8,7},{9,8},{10,9... | collective-permute-start | bytes 3145736 | tf_op jit(solution)/shard_map/ppermute | solution.py:9
  60.5 4.0 %fusion.32 = (f32[128]{0:T(128)S(1)}, f32[1024]{0:T(1024)S(1)}) fusion(bf16[1024,4096]{0,1:T(8,128)(2,1)S(1)} %bitcast.59, bf16[128,4096]{1,0:T(8,128)(2,1)} %collective-permute-done.4, f32[1024]{0:T(1024)S(1)} %broadcast_bitcast_fusion.3, s32[128]{0:T(128)S(1)} %get-tuple-element.33, s32[1024]{0:T(1024)S(1)} %copy-done.4), kind=kOutput, calls=%fused_computation.73 | convolution fusion | flops 1074658176 | bytes 9450496 | tf_op jit(solution)/shard_map/dot_general | solution.py:33
  64.7 2.7 %fusion.27 = (f32[128]{0:T(128)S(1)}, f32[1024]{0:T(1024)S(1)}) fusion(bf16[1024,4096]{0,1:T(8,128)(2,1)S(1)} %bitcast.60, bf16[128,4096]{1,0:T(8,128)(2,1)S(1)} %collective-permute-done, f32[1024]{0:T(1024)S(1)} %broadcast_bitcast_fusion.7, s32[128]{0:T(128)S(1)} %get-tuple-element.29, s32[1024]{0:T(1024)S(1)} %copy-done.4), kind=kOutput, calls=%fused_computation.68 | convolution fusion | flops 1074658176 | bytes 9450496 | tf_op jit(solution)/shard_map/dot_general | solution.py:33
  68.0 5.3 %collective-permute-done.5 = bf16[128,4096]{1,0:T(8,128)(2,1)S(1)} collective-permute-done((bf16[128,4096]{1,0:T(8,128)(2,1)}, bf16[128,4096]{1,0:T(8,128)(2,1)S(1)}, u32[]{:S(2)}, u32[]{:S(2)}) %collective-permute-start.5) | collective-permute-done | bytes 1048608 | tf_op jit(solution)/shard_map/ppermute | solution.py:9
  73.3 5.4 %collective-permute-start.6 = (bf16[128,4096]{1,0:T(8,128)(2,1)S(1)}, bf16[128,4096]{1,0:T(8,128)(2,1)S(1)}, u32[]{:S(2)}, u32[]{:S(2)}) collective-permute-start(bf16[128,4096]{1,0:T(8,128)(2,1)S(1)} %collective-permute-done.5), channel_id=1, source_target_pairs={{0,1},{1,2},{2,3},{3,4},{4,5},{5,6},{6,7},{7,8},{8,9},{9,10},{10,1... | collective-permute-start | bytes 3145736 | tf_op jit(solution)/shard_map/ppermute | solution.py:9
  78.7 2.8 %fusion.33 = (f32[128]{0:T(128)S(1)}, f32[1024]{0:T(1024)S(1)}) fusion(bf16[1024,4096]{0,1:T(8,128)(2,1)S(1)} %bitcast.61, bf16[128,4096]{1,0:T(8,128)(2,1)S(1)} %collective-permute-done.5, f32[1024]{0:T(1024)S(1)} %broadcast_bitcast_fusion.2, s32[128]{0:T(128)S(1)} %get-tuple-element.32, s32[1024]{0:T(1024)S(1)} %copy-done.4), kind=kOutput, calls=%fused_computation.74 | convolution fusion | flops 1074658176 | bytes 9450496 | tf_op jit(solution)/shard_map/dot_general | solution.py:33
  81.4 18.1 %collective-permute-start.13 = (f32[128]{0:T(128)S(1)}, f32[128]{0:T(128)S(1)}, u32[]{:S(2)}, u32[]{:S(2)}) collective-permute-start(f32[128]{0:T(128)S(1)} %get-tuple-element.14), channel_id=1, source_target_pairs={{0,14},{1,15},{2,0},{3,1},{4,2},{5,3},{6,4},{7,5},{8,6},{9,7},{10,... | collective-permute-start | bytes 1544 | tf_op jit(solution)/shard_map/ppermute | solution.py:9
  99.6 2.8 %fusion.29 = (f32[128]{0:T(128)S(1)}, f32[1024]{0:T(1024)S(1)}) fusion(bf16[1024,4096]{0,1:T(8,128)(2,1)S(1)} %bitcast.62, bf16[128,4096]{1,0:T(8,128)(2,1)S(1)} %collective-permute-done.1, f32[1024]{0:T(1024)S(1)} %broadcast_bitcast_fusion.6, s32[128]{0:T(128)S(1)} %get-tuple-element.36, s32[1024]{0:T(1024)S(1)} %copy-done.4), kind=kOutput, calls=%fused_computation.70 | convolution fusion | flops 1074658176 | bytes 9450496 | tf_op jit(solution)/shard_map/dot_general | solution.py:33
  103.4 3.5 %collective-permute-start.3 = (bf16[128,4096]{1,0:T(8,128)(2,1)S(1)}, bf16[128,4096]{1,0:T(8,128)(2,1)S(1)}, u32[]{:S(2)}, u32[]{:S(2)}) collective-permute-start(bf16[128,4096]{1,0:T(8,128)(2,1)S(1)} %collective-permute-done.2), channel_id=1, source_target_pairs={{0,15},{1,0},{2,1},{3,2},{4,3},{5,4},{6,5},{7,6},{8,7},{9,8},{10,9... | collective-permute-start | bytes 3145736 | tf_op jit(solution)/shard_map/ppermute | solution.py:9
  106.8 2.8 %fusion.34 = (f32[128]{0:T(128)S(1)}, f32[1024]{0:T(1024)S(1)}) fusion(bf16[1024,4096]{0,1:T(8,128)(2,1)S(1)} %bitcast.63, bf16[128,4096]{1,0:T(8,128)(2,1)S(1)} %collective-permute-done.6, f32[1024]{0:T(1024)S(1)} %broadcast_bitcast_fusion.1, s32[128]{0:T(128)S(1)} %get-tuple-element.31, s32[1024]{0:T(1024)S(1)} %copy-done.4), kind=kOutput, calls=%fused_computation.75 | convolution fusion | flops 1074658176 | bytes 9450496 | tf_op jit(solution)/shard_map/dot_general | solution.py:33
  109.6 2.8 %fusion.30 = (f32[128]{0:T(128)S(1)}, f32[1024]{0:T(1024)S(1)}) fusion(bf16[1024,4096]{0,1:T(8,128)(2,1)S(1)} %bitcast.64, bf16[128,4096]{1,0:T(8,128)(2,1)S(1)} %collective-permute-done.2, f32[1024]{0:T(1024)S(1)} %broadcast_bitcast_fusion.5, s32[128]{0:T(128)S(1)} %get-tuple-element.35, s32[1024]{0:T(1024)S(1)} %copy-done.4), kind=kOutput, calls=%fused_computation.71 | convolution fusion | flops 1074658176 | bytes 9450496 | tf_op jit(solution)/shard_map/dot_general | solution.py:33
  112.4 7.0 %collective-permute-done.7 = bf16[128,4096]{1,0:T(8,128)(2,1)S(1)} collective-permute-done((bf16[128,4096]{1,0:T(8,128)(2,1)S(1)}, bf16[128,4096]{1,0:T(8,128)(2,1)S(1)}, u32[]{:S(2)}, u32[]{:S(2)}) %collective-permute-start.7) | collective-permute-done | bytes 1048608 | tf_op jit(solution)/shard_map/ppermute | solution.py:9
  119.4 11.0 %collective-permute-start.9 = (f32[128]{0:T(128)S(1)}, f32[128]{0:T(128)S(1)}, u32[]{:S(2)}, u32[]{:S(2)}) collective-permute-start(f32[128]{0:T(128)S(1)} %get-tuple-element.6), channel_id=1, source_target_pairs={{0,2},{1,3},{2,4},{3,5},{4,6},{5,7},{6,8},{7,9},{8,10},{9,11},{10,... | collective-permute-start | bytes 1544 | tf_op jit(solution)/shard_map/ppermute | solution.py:9
  130.4 2.8 %fusion.35 = (f32[128]{0:T(128)S(1)}, f32[1024]{0:T(1024)S(1)}) fusion(bf16[1024,4096]{0,1:T(8,128)(2,1)S(1)} %bitcast.65, bf16[128,4096]{1,0:T(8,128)(2,1)S(1)} %collective-permute-done.7, f32[1024]{0:T(1024)S(1)} %broadcast_bitcast_fusion, s32[128]{0:T(128)S(1)} %get-tuple-element.30, s32[1024]{0:T(1024)S(1)} %copy-done.4), kind=kOutput, calls=%fused_computation.76 | convolution fusion | flops 1074658176 | bytes 9450496 | tf_op jit(solution)/shard_map/dot_general | solution.py:33
  135.0 2.8 %fusion.31 = (f32[128]{0:T(128)S(1)}, f32[1024]{0:T(1024)S(1)}) fusion(bf16[1024,4096]{0,1:T(8,128)(2,1)S(1)} %bitcast.66, bf16[128,4096]{1,0:T(8,128)(2,1)S(1)} %collective-permute-done.3, f32[1024]{0:T(1024)S(1)} %broadcast_bitcast_fusion.4, s32[128]{0:T(128)S(1)} %get-tuple-element.34, s32[1024]{0:T(1024)S(1)} %copy-done.4), kind=kOutput, calls=%fused_computation.72 | convolution fusion | flops 1074658176 | bytes 9450496 | tf_op jit(solution)/shard_map/dot_general | solution.py:33
  137.8 3.0 %collective-permute-start.15 = (f32[128]{0:T(128)S(1)}, f32[128]{0:T(128)S(1)}, u32[]{:S(2)}, u32[]{:S(2)}) collective-permute-start(f32[128]{0:T(128)S(1)} %get-tuple-element.18), channel_id=1, source_target_pairs={{0,12},{1,13},{2,14},{3,15},{4,0},{5,1},{6,2},{7,3},{8,4},{9,5},{1... | collective-permute-start | bytes 1544 | tf_op jit(solution)/shard_map/ppermute | solution.py:9
  142.6 3.6 %collective-permute-done.11 = f32[128]{0:T(128)S(1)} collective-permute-done((f32[128]{0:T(128)S(1)}, f32[128]{0:T(128)S(1)}, u32[]{:S(2)}, u32[]{:S(2)}) %collective-permute-start.11) | collective-permute-done | bytes 544 | tf_op jit(solution)/shard_map/ppermute | solution.py:9
  (46 shorter events, 8.2 us)
Async XLA Ops:
  0.6 55.4 %collective-permute-start.4 = (bf16[128,4096]{1,0:T(8,128)(2,1)}, bf16[128,4096]{1,0:T(8,128)(2,1)}, u32[]{:S(2)}, u32[]{:S(2)}) collective-permute-start(bf16[128,4096]{1,0:T(8,128)(2,1)} %param.11), channel_id=1, source_target_pairs={{0,1},{1,2},{2,3},{3,4},{4,5},{5,6},{6,7},{7,8},{8,9},{9,10},{10,1... | collective-permute-start | bytes 3145736 | tf_op jit(solution)/shard_map/ppermute | solution.py:9
  1.1 54.9 %collective-permute-start = (bf16[128,4096]{1,0:T(8,128)(2,1)}, bf16[128,4096]{1,0:T(8,128)(2,1)S(1)}, u32[]{:S(2)}, u32[]{:S(2)}) collective-permute-start(bf16[128,4096]{1,0:T(8,128)(2,1)} %param.11), channel_id=1, source_target_pairs={{0,15},{1,0},{2,1},{3,2},{4,3},{5,4},{6,5},{7,6},{8,7},{9,8},{10,9... | collective-permute-start | bytes 3145736 | tf_op jit(solution)/shard_map/ppermute | solution.py:9
  30.3 18.4 %copy-start.1 = (s32[8,9]{1,0:T(8,128)S(1)}, s32[8,9]{1,0:T(8,128)}, u32[]{:S(2)}) copy-start(s32[8,9]{1,0:T(8,128)} %param.13) | copy-start | bytes 868
  30.3 19.2 %copy-start.2 = (s32[2048]{0:T(1024)S(1)}, s32[2048]{0:T(1024)}, u32[]{:S(2)}) copy-start(s32[2048]{0:T(1024)} %param.12) | copy-start | bytes 24580
  30.3 19.4 %copy-start.3 = (bf16[128,4096]{1,0:T(8,128)(2,1)S(1)}, bf16[128,4096]{1,0:T(8,128)(2,1)}, u32[]{:S(2)}) copy-start(bf16[128,4096]{1,0:T(8,128)(2,1)} %param.11) | copy-start | bytes 3145732
  30.3 19.4 %copy-start.4 = (s32[1024]{0:T(1024)S(1)}, s32[1024]{0:T(1024)}, u32[]{:S(2)}) copy-start(s32[1024]{0:T(1024)} %param.10) | copy-start | bytes 12292
  49.5 10.9 %copy-start = (bf16[1024,64,64]{0,2,1:T(8,128)(2,1)S(1)}, bf16[1024,64,64]{0,2,1:T(8,128)(2,1)}, u32[]{:S(2)}) copy-start(bf16[1024,64,64]{0,2,1:T(8,128)(2,1)} %copy.13) | copy-start | bytes 25165828
  56.0 17.3 %collective-permute-start.5 = (bf16[128,4096]{1,0:T(8,128)(2,1)}, bf16[128,4096]{1,0:T(8,128)(2,1)S(1)}, u32[]{:S(2)}, u32[]{:S(2)}) collective-permute-start(bf16[128,4096]{1,0:T(8,128)(2,1)} %collective-permute-done.4), channel_id=1, source_target_pairs={{0,1},{1,2},{2,3},{3,4},{4,5},{5,6},{6,7},{7,8},{8,9},{9,10},{10,1... | collective-permute-start | bytes 3145736 | tf_op jit(solution)/shard_map/ppermute | solution.py:9
  56.1 22.6 %collective-permute-start.1 = (bf16[128,4096]{1,0:T(8,128)(2,1)S(1)}, bf16[128,4096]{1,0:T(8,128)(2,1)S(1)}, u32[]{:S(2)}, u32[]{:S(2)}) collective-permute-start(bf16[128,4096]{1,0:T(8,128)(2,1)S(1)} %collective-permute-done), channel_id=1, source_target_pairs={{0,15},{1,0},{2,1},{3,2},{4,3},{5,4},{6,5},{7,6},{8,7},{9,8},{10,9... | collective-permute-start | bytes 3145736 | tf_op jit(solution)/shard_map/ppermute | solution.py:9
  64.5 73.3 %collective-permute-start.12 = (f32[128]{0:T(128)S(1)}, f32[128]{0:T(128)S(1)}, u32[]{:S(2)}, u32[]{:S(2)}) collective-permute-start(f32[128]{0:T(128)S(1)} %get-tuple-element.12), channel_id=1, source_target_pairs={{0,15},{1,0},{2,1},{3,2},{4,3},{5,4},{6,5},{7,6},{8,7},{9,8},{10,9... | collective-permute-start | bytes 1544 | tf_op jit(solution)/shard_map/ppermute | solution.py:9
  67.5 70.4 %collective-permute-start.8 = (f32[128]{0:T(128)S(1)}, f32[128]{0:T(128)S(1)}, u32[]{:S(2)}, u32[]{:S(2)}) collective-permute-start(f32[128]{0:T(128)S(1)} %get-tuple-element.2), channel_id=1, source_target_pairs={{0,1},{1,2},{2,3},{3,4},{4,5},{5,6},{6,7},{7,8},{8,9},{9,10},{10,1... | collective-permute-start | bytes 1544 | tf_op jit(solution)/shard_map/ppermute | solution.py:9
  73.3 29.1 %collective-permute-start.6 = (bf16[128,4096]{1,0:T(8,128)(2,1)S(1)}, bf16[128,4096]{1,0:T(8,128)(2,1)S(1)}, u32[]{:S(2)}, u32[]{:S(2)}) collective-permute-start(bf16[128,4096]{1,0:T(8,128)(2,1)S(1)} %collective-permute-done.5), channel_id=1, source_target_pairs={{0,1},{1,2},{2,3},{3,4},{4,5},{5,6},{6,7},{7,8},{8,9},{9,10},{10,1... | collective-permute-start | bytes 3145736 | tf_op jit(solution)/shard_map/ppermute | solution.py:9
  78.7 24.7 %collective-permute-start.2 = (bf16[128,4096]{1,0:T(8,128)(2,1)S(1)}, bf16[128,4096]{1,0:T(8,128)(2,1)S(1)}, u32[]{:S(2)}, u32[]{:S(2)}) collective-permute-start(bf16[128,4096]{1,0:T(8,128)(2,1)S(1)} %collective-permute-done.1), channel_id=1, source_target_pairs={{0,15},{1,0},{2,1},{3,2},{4,3},{5,4},{6,5},{7,6},{8,7},{9,8},{10,9... | collective-permute-start | bytes 3145736 | tf_op jit(solution)/shard_map/ppermute | solution.py:9
  81.4 59.4 %collective-permute-start.13 = (f32[128]{0:T(128)S(1)}, f32[128]{0:T(128)S(1)}, u32[]{:S(2)}, u32[]{:S(2)}) collective-permute-start(f32[128]{0:T(128)S(1)} %get-tuple-element.14), channel_id=1, source_target_pairs={{0,14},{1,15},{2,0},{3,1},{4,2},{5,3},{6,4},{7,5},{8,6},{9,7},{10,... | collective-permute-start | bytes 1544 | tf_op jit(solution)/shard_map/ppermute | solution.py:9
  102.3 17.1 %collective-permute-start.7 = (bf16[128,4096]{1,0:T(8,128)(2,1)S(1)}, bf16[128,4096]{1,0:T(8,128)(2,1)S(1)}, u32[]{:S(2)}, u32[]{:S(2)}) collective-permute-start(bf16[128,4096]{1,0:T(8,128)(2,1)S(1)} %collective-permute-done.6), channel_id=1, source_target_pairs={{0,1},{1,2},{2,3},{3,4},{4,5},{5,6},{6,7},{7,8},{8,9},{9,10},{10,1... | collective-permute-start | bytes 3145736 | tf_op jit(solution)/shard_map/ppermute | solution.py:9
  103.4 29.8 %collective-permute-start.3 = (bf16[128,4096]{1,0:T(8,128)(2,1)S(1)}, bf16[128,4096]{1,0:T(8,128)(2,1)S(1)}, u32[]{:S(2)}, u32[]{:S(2)}) collective-permute-start(bf16[128,4096]{1,0:T(8,128)(2,1)S(1)} %collective-permute-done.2), channel_id=1, source_target_pairs={{0,15},{1,0},{2,1},{3,2},{4,3},{5,4},{6,5},{7,6},{8,7},{9,8},{10,9... | collective-permute-start | bytes 3145736 | tf_op jit(solution)/shard_map/ppermute | solution.py:9
  119.4 22.0 %collective-permute-start.9 = (f32[128]{0:T(128)S(1)}, f32[128]{0:T(128)S(1)}, u32[]{:S(2)}, u32[]{:S(2)}) collective-permute-start(f32[128]{0:T(128)S(1)} %get-tuple-element.6), channel_id=1, source_target_pairs={{0,2},{1,3},{2,4},{3,5},{4,6},{5,7},{6,8},{7,9},{8,10},{9,11},{10,... | collective-permute-start | bytes 1544 | tf_op jit(solution)/shard_map/ppermute | solution.py:9
  133.2 8.3 %collective-permute-start.14 = (f32[128]{0:T(128)S(1)}, f32[128]{0:T(128)S(1)}, u32[]{:S(2)}, u32[]{:S(2)}) collective-permute-start(f32[128]{0:T(128)S(1)} %get-tuple-element.16), channel_id=1, source_target_pairs={{0,13},{1,14},{2,15},{3,0},{4,1},{5,2},{6,3},{7,4},{8,5},{9,6},{10... | collective-permute-start | bytes 1544 | tf_op jit(solution)/shard_map/ppermute | solution.py:9
  137.8 4.8 %collective-permute-start.10 = (f32[128]{0:T(128)S(1)}, f32[128]{0:T(128)S(1)}, u32[]{:S(2)}, u32[]{:S(2)}) collective-permute-start(f32[128]{0:T(128)S(1)} %get-tuple-element.8), channel_id=1, source_target_pairs={{0,3},{1,4},{2,5},{3,6},{4,7},{5,8},{6,9},{7,10},{8,11},{9,12},{10... | collective-permute-start | bytes 1544 | tf_op jit(solution)/shard_map/ppermute | solution.py:9
  137.8 4.7 %collective-permute-start.15 = (f32[128]{0:T(128)S(1)}, f32[128]{0:T(128)S(1)}, u32[]{:S(2)}, u32[]{:S(2)}) collective-permute-start(f32[128]{0:T(128)S(1)} %get-tuple-element.18), channel_id=1, source_target_pairs={{0,12},{1,13},{2,14},{3,15},{4,0},{5,1},{6,2},{7,3},{8,4},{9,5},{1... | collective-permute-start | bytes 1544 | tf_op jit(solution)/shard_map/ppermute | solution.py:9
  140.9 5.3 %collective-permute-start.11 = (f32[128]{0:T(128)S(1)}, f32[128]{0:T(128)S(1)}, u32[]{:S(2)}, u32[]{:S(2)}) collective-permute-start(f32[128]{0:T(128)S(1)} %get-tuple-element.10), channel_id=1, source_target_pairs={{0,4},{1,5},{2,6},{3,7},{4,8},{5,9},{6,10},{7,11},{8,12},{9,13},{1... | collective-permute-start | bytes 1544 | tf_op jit(solution)/shard_map/ppermute | solution.py:9
where the time goes:
time: 147 us
  starting transfers between devices  54.7 us (37%)
  matrix products  40.1 us (27%)
  local copies, waits for them, and re-layouts  30.1 us (20%)
  waiting for transfers between devices  17 us (12%)
  other arithmetic  3.93 us (3%)
    ppermute x16, starting transfers between devices, passed_along(): lax.ppermute(value, axis, [(i, (i + by) % devices) for i in range(devices)])  54.7 us
    dot_general x9, matrix products, score_block(): jnp.dot(sketch, visiting.T, preferred_element_type=jnp.float32) * inv  29.6 us
    convert_element_type x1, local copies, waits for them, and re-layouts, per_device(): sketch = sketch.reshape(train_rows, width).astype(jnp.bfloat16)  18.4 us
    ppermute x16, waiting for transfers between devices, passed_along(): lax.ppermute(value, axis, [(i, (i + by) % devices) for i in range(devices)])  17 us
    dot_general x1, matrix products, per_device(): jnp.einsum('rti,rto->rio', left, out_factors, preferred_element_type=jnp....  10.6 us
    unnamed x11, local copies, waits for them, and re-layouts  6.19 us
    select_n x1, local copies, waits for them, and re-layouts, per_device(): left = jnp.where(live[:, :, None], in_factors, jnp.zeros_like(in_factors))  4.9 us
  transfers between devices with their start and end apart: 16, of which 4 were waited for; matrix products, arithmetic and copies ran while one was open for 50% of the time, Pallas kernels for 0%

commit v1 on v0

v1 whole, which is shorter than its diff:
```python
import jax
import jax.numpy as jnp
from jax import lax
from jax.experimental import pallas as pl
from jax.experimental.pallas import tpu as pltpu
from jax.sharding import PartitionSpec as P

HALVES = 2
PLANE = 4
GROUP = 4

OWN, CORE, SIDE, CORE_SIDE, FIRST, SECOND, DIAG, CORE_DIAG, CORE_PLANE = range(9)
SLOTS = 9


def kernel(
    in_hbm, out_hbm, counts_ref, tclus_ref, q_hbm, qclus_ref, mask_ref,
    train_ref, query_ref,
    in_raw, out_raw, in_f32, out_f32, sketch, blocks, qacc, tacc, qout, qin,
    load_sem, own_sem, send_sem, recv_sem, back_send, back_recv,
):
    n = lax.axis_size("blk")
    b = lax.axis_index("blk")
    place = lax.rem(b, PLANE)
    side = place // 2
    core = lax.rem(place, 2)
    slots, rin, rows = in_f32.shape
    rout = out_f32.shape[1]
    tile = query_ref.shape[1]
    band = mask_ref.shape[1]
    reach = (band - 1) // 2
    width = rin * rout
    piece = tile // HALVES
    scale = 1.0 / width**0.5 / 32.0

    to_core = b + 1 - 2 * core
    to_side = b + 2 - 4 * side
    above = lax.rem(b + PLANE, n)
    below = lax.rem(b + n - PLANE, n)
    to_first = side * above + (1 - side) * below
    to_second = side * below + (1 - side) * above
    offsets = {
        OWN: 0,
        CORE: 1 - 2 * core,
        SIDE: 2 - 4 * side,
        CORE_SIDE: 3 - 2 * place,
        FIRST: 4 - 8 * side,
        SECOND: 8 * side - 4,
        DIAG: 4 * side - 2,
        CORE_DIAG: 8 * side - 1 - 2 * place,
        CORE_PLANE: 6 * core - 3,
    }

    load_in = pltpu.make_async_copy(in_hbm, in_raw, load_sem.at[0])
    load_out = pltpu.make_async_copy(out_hbm, out_raw, load_sem.at[1])
    load_in.start()
    load_out.start()

    barrier = pltpu.get_barrier_semaphore()
    for step in range(1, reach + 1):
        for other in (lax.rem(b + step, n), lax.rem(b + n - step, n)):
            pl.semaphore_signal(
                barrier, inc=1, device_id={"blk": other}, device_id_type=pl.DeviceIdType.MESH
            )
    pl.semaphore_wait(barrier, 2 * reach)

    def own(h):
        return q_hbm.at[pl.ds(h * piece, piece), :]

    def send(src, slot, h, device):
        return pltpu.make_async_remote_copy(
            src_ref=src,
            dst_ref=blocks.at[h, slot],
            send_sem=send_sem.at[slot, h],
            recv_sem=recv_sem.at[slot, h],
            device_id={"blk": device},
            device_id_type=pl.DeviceIdType.MESH,
        )

    halves = range(HALVES)
    first = [send(own(h), FIRST, h, to_first) for h in halves]
    aside = [send(own(h), SIDE, h, to_side) for h in halves]
    twin = [send(own(h), CORE, h, to_core) for h in halves]
    second = [send(own(h), SECOND, h, to_second) for h in halves]
    diag = [send(blocks.at[h, FIRST], DIAG, h, to_side) for h in halves]
    twin_side = [send(blocks.at[h, SIDE], CORE_SIDE, h, to_core) for h in halves]
    twin_diag = [send(blocks.at[h, DIAG], CORE_DIAG, h, to_core) for h in halves]
    plane_first = [send(blocks.at[h, FIRST], CORE_PLANE, h, to_core) for h in halves]
    plane_second = [send(blocks.at[h, SECOND], CORE_PLANE, h, to_core) for h in halves]
    mine = [pltpu.make_async_copy(own(h), blocks.at[h, OWN], own_sem.at[h]) for h in halves]
    for h in halves:
        first[h].start()
        aside[h].start()
    for h in halves:
        twin[h].start()
        mine[h].start()

    load_in.wait()
    load_out.wait()
    counts = counts_ref[...]

    @pl.loop(0, slots)
    def _(t):
        live = counts > t
        value = in_raw[t].astype(jnp.float32)
        in_f32[t] = jnp.where(live, value, 0.0)
        out_f32[t] = out_raw[t].astype(jnp.float32)

    @pl.loop(0, rows // 128)
    def _(chunk):
        lanes = pl.ds(pl.multiple_of(chunk * 128, 128), 128)

        @pl.loop(0, rin // 8)
        def _(group):
            eight = pl.ds(pl.multiple_of(group * 8, 8), 8)
            for low in range(0, 8, GROUP):
                sums = [None] * GROUP
                for t in range(slots):
                    right = out_f32[t, :, lanes]
                    left = in_f32[t, eight, lanes]
                    for g in range(GROUP):
                        row = left[low + g : low + g + 1]
                        term = row * right
                        sums[g] = term if t == 0 else sums[g] + term
                for g in range(GROUP):
                    at = pl.multiple_of(group * (8 * rout) + (low + g) * rout, rout)
                    sketch[pl.ds(at, rout), lanes] = sums[g].astype(jnp.bfloat16)

    for h in halves:
        first[h].wait_send()
    for h in halves:
        second[h].start()
    for h in halves:
        first[h].wait_recv()
        diag[h].start()

        @pl.when(side == core)
        def _(h=h):
            plane_first[h].start()

        aside[h].wait_recv()
        twin_side[h].start()

    tacc[...] = jnp.zeros_like(tacc)
    qacc[...] = jnp.zeros_like(qacc)

    def score(h, low, high):
        clusters = []
        for slot in range(low, high):
            source = lax.rem(b + offsets[slot] + n, n)
            row = qclus_ref[source].astype(jnp.float32)
            full = jnp.transpose(jnp.broadcast_to(row, (tile, tile)))
            clusters.append(full[h * piece : (h + 1) * piece])

        @pl.loop(0, rows // 256)
        def _(step):
            lanes = pl.ds(pl.multiple_of(step * 256, 256), 256)
            query = blocks[h, low:high].reshape((high - low) * piece, width)
            dots = jnp.dot(query, sketch[:, lanes], preferred_element_type=jnp.float32)
            for part in range(2):
                tile_lanes = pl.ds(pl.multiple_of(step * 256 + part * 128, 128), 128)
                tclus = tclus_ref[:, tile_lanes].astype(jnp.float32)
                total = tacc[:, tile_lanes]
                for i, slot in enumerate(range(low, high)):
                    open_tile = mask_ref[step * 2 + part, offsets[slot] + reach]
                    wanted = jnp.where(open_tile > 0, tclus, -1.0)
                    got = dots[i * piece : (i + 1) * piece, part * 128 : part * 128 + 128]
                    got = jnp.where(clusters[i] == wanted, jnp.maximum(got, 0.0), 0.0)
                    total = total + jnp.sum(got.reshape(piece // 8, 8, 128), axis=0)
                    qacc[slot, h * piece : (h + 1) * piece, :] += got
                tacc[:, tile_lanes] = total

    def back(slot):
        return pltpu.make_async_remote_copy(
            src_ref=qout.at[slot],
            dst_ref=qin.at[offsets[slot] + reach],
            send_sem=back_send.at[slot],
            recv_sem=back_recv.at[offsets[slot] + reach],
            device_id={"blk": lax.rem(b + offsets[slot] + n, n)},
            device_id_type=pl.DeviceIdType.MESH,
        )

    def give_back(low, high):
        for slot in range(low, high):
            qout[slot] = jnp.sum(jnp.transpose(qacc[slot]), axis=0, keepdims=True)
            if slot != OWN:
                back(slot).start()

    for h in halves:
        mine[h].wait()
        twin[h].wait_recv()
        twin_side[h].wait_recv()
        score(h, OWN, SECOND)
    give_back(OWN, SECOND)

    for h in halves:
        second[h].wait_recv()

        @pl.when(side != core)
        def _(h=h):
            plane_second[h].start()

        diag[h].wait_recv()
        twin_diag[h].start()
        twin_diag[h].wait_recv()
        plane_first[h].wait_recv()
        score(h, SECOND, SLOTS)
    give_back(SECOND, SLOTS)

    train_ref[...] = jnp.sum(tacc[...], axis=0, keepdims=True) * scale
    total = qout[OWN]
    for column in range(band):
        if column != reach:
            pltpu.make_async_remote_copy(
                src_ref=qout.at[0],
                dst_ref=qin.at[column],
                send_sem=back_send.at[0],
                recv_sem=back_recv.at[column],
                device_id={"blk": to_core},
                device_id_type=pl.DeviceIdType.MESH,
            ).wait_recv()
            total = total + qin[column]
    query_ref[...] = total * scale

    for h in halves:
        for copy in (aside, twin, second, diag, twin_side, twin_diag, plane_first):
            copy[h].wait_send()
    for slot in range(1, SLOTS):
        back(slot).wait_send()


def per_device(
    in_factors, out_factors, token_counts, train_cluster, queries, query_cluster, pair_mask
):
    rows, slots, rin = in_factors.shape
    rout = out_factors.shape[2]
    tile, width = queries.shape
    nblocks = lax.axis_size("blk")
    band = pair_mask.shape[1]
    piece = tile // HALVES
    vmem = pl.BlockSpec(memory_space=pltpu.VMEM)
    anywhere = pl.BlockSpec(memory_space=pl.ANY)
    train, query = pl.pallas_call(
        kernel,
        out_shape=(
            jax.ShapeDtypeStruct((1, rows), jnp.float32),
            jax.ShapeDtypeStruct((1, tile), jnp.float32),
        ),
        in_specs=[
            anywhere, anywhere, vmem, vmem, anywhere, vmem,
            pl.BlockSpec(memory_space=pltpu.SMEM),
        ],
        out_specs=(vmem, vmem),
        scratch_shapes=[
            pltpu.VMEM((slots, rin, rows), jnp.bfloat16),
            pltpu.VMEM((slots, rout, rows), jnp.bfloat16),
            pltpu.VMEM((slots, rin, rows), jnp.float32),
            pltpu.VMEM((slots, rout, rows), jnp.float32),
            pltpu.VMEM((width, rows), jnp.bfloat16),
            pltpu.VMEM((HALVES, SLOTS, piece, width), jnp.bfloat16),
            pltpu.VMEM((SLOTS, tile, 128), jnp.float32),
            pltpu.VMEM((8, rows), jnp.float32),
            pltpu.VMEM((SLOTS, 1, tile), jnp.float32),
            pltpu.VMEM((band, 1, tile), jnp.float32),
            pltpu.SemaphoreType.DMA((2,)),
            pltpu.SemaphoreType.DMA((HALVES,)),
            pltpu.SemaphoreType.DMA((SLOTS, HALVES)),
            pltpu.SemaphoreType.DMA((SLOTS, HALVES)),
            pltpu.SemaphoreType.DMA((SLOTS,)),
            pltpu.SemaphoreType.DMA((band,)),
        ],
        compiler_params=pltpu.CompilerParams(
            collective_id=0, has_side_effects=True, vmem_limit_bytes=56 * 2**20
        ),
        name="score_blocks",
    )(
        jnp.transpose(in_factors, (1, 2, 0)),
        jnp.transpose(out_factors, (1, 2, 0)),
        token_counts.reshape(1, rows),
        train_cluster.reshape(1, rows),
        queries,
        query_cluster.reshape(nblocks, 1, tile),
        pair_mask,
    )
    return train.reshape(rows), query.reshape(tile)


def solution(mesh):
    placed = (
        P(("groups", "blk"), None, None),
        P(("groups", "blk"), None, None),
        P(("groups", "blk")),
        P(("groups", "blk")),
        P(("groups", "blk"), None),
        P("groups"),
        P(("groups", "blk"), None),
    )
    return jax.shard_map(
        per_device,
        mesh=mesh,
        in_specs=placed,
        out_specs=(P(("groups", "blk")), P(("groups", "blk"))),
        check_vma=False,
    )
```

time: 147 us -> 67.8 us (0.46)
  Pallas kernels: 0 us -> 64.5 us
  starting transfers between devices: 54.7 us -> 0 us
  matrix products: 40.1 us -> 0 us
  local copies, waits for them, and re-layouts: 30.1 us -> 2.4 us
  waiting for transfers between devices: 17 us -> 0 us
  other arithmetic: 3.93 us -> 0 us
    pallas_call x0 -> x1, Pallas kernels: none -> 64.5 us  [per_device(): pl.pallas_call(kernel, out_shape=(jax.ShapeDtypeStruct((1, rows), jnp.flo...]
    ppermute x16 -> x0, starting transfers between devices: 54.7 us -> none  [passed_along(): lax.ppermute(value, axis, [(i, (i + by) % devices) for i in range(devices)])]
    dot_general x10 -> x0, matrix products: 40.1 us -> none  [the longest x9 29.6 us: score_block(): jnp.dot(sketch, visiting.T, preferred_element_type=jnp.float32) * inv]
    convert_element_type x10 -> x0, local copies, waits for them, and re-layouts: 19 us -> none  [the longest x1 18.4 us: per_device(): sketch = sketch.reshape(train_rows, width).astype(jnp.bfloat16)]
    ppermute x16 -> x0, waiting for transfers between devices: 17 us -> none  [passed_along(): lax.ppermute(value, axis, [(i, (i + by) % devices) for i in range(devices)])]
    select_n x1 -> x0, local copies, waits for them, and re-layouts: 4.9 us -> none  [per_device(): left = jnp.where(live[:, :, None], in_factors, jnp.zeros_like(in_factors))]
    unnamed x11 -> x2, local copies, waits for them, and re-layouts: 6.19 us -> 2.4 us
    select_n x1 -> x0, other arithmetic: 1.78 us -> none  [per_device(): left = jnp.where(live[:, :, None], in_factors, jnp.zeros_like(in_factors))]
  transfers between devices with their start and end apart: 16 -> 0, of which waited for: 4 -> 0; matrix products, arithmetic and copies ran while one was open for 50% -> 0% of each run, Pallas kernels for 0% -> 0%
where the time goes in v1:
time: 67.8 us; the launch traced here: 67.5 us
  Pallas kernels  64.5 us (95%)
  local copies, waits for them, and re-layouts  2.4 us (4%)
    pallas_call x1, Pallas kernels, per_device(): pl.pallas_call(kernel, out_shape=(jax.ShapeDtypeStruct((1, rows), jnp.flo...  64.5 us
    unnamed x2, local copies, waits for them, and re-layouts  2.4 us

profile of v1, /device:TPU:0, one launch (start us, length us, event | category | flops | bytes accessed | tf_op | source)
XLA Modules:
  0.0 67.5 jit_solution(3704078101782302365)
XLA Ops:
  0.6 64.5 %score_blocks.1 = (f32[1,1024]{1,0:T(1,128)}, f32[1,128]{1,0:T(1,128)}) custom-call(bf16[16,64,1024]{2,1,0:T(8,128)(2,1)} %bitcast.7, bf16[16,64,1024]{2,1,0:T(8,128)(2,1)} %bitcast.8, s32[1,1024]{1,0:T(1,128)} %bitcast.11, s32[1,1024]{1,0:T(1,128)} %bitcast.12, bf16[128,4096]{1,0:T(8,128)(2,1)} %q_hbm.1, s32[16,1,128]{2,1,0:T(1,128)} %bitcast.9, ...), custom_call_target="tpu_custom_call" | custom-call | tf_op jit(solution)/shard_map/score_blocks/pallas_call | solution.py:243
  65.1 1.3 %copy.11 = f32[1024]{0:T(1024)} copy(f32[1024]{0:T(1024)} %bitcast.10) | data formatting | bytes 8192
  66.4 1.1 %copy.12 = f32[128]{0:T(128)} copy(f32[128]{0:T(128)} %bitcast.13) | data formatting | bytes 1024

commit v2 on v1

--- a/solution.py
+++ b/solution.py
@@ -5,7 +5,8 @@
 from jax.experimental.pallas import tpu as pltpu
 from jax.sharding import PartitionSpec as P
 
-HALVES = 2
+PIECES = 4
+AHEAD = 4
 PLANE = 4
 GROUP = 4
 
@@ -30,7 +31,7 @@
     band = mask_ref.shape[1]
     reach = (band - 1) // 2
     width = rin * rout
-    piece = tile // HALVES
+    piece = tile // PIECES
     scale = 1.0 / width**0.5 / 32.0
 
     to_core = b + 1 - 2 * core
@@ -77,21 +78,21 @@
             device_id_type=pl.DeviceIdType.MESH,
         )
 
-    halves = range(HALVES)
-    first = [send(own(h), FIRST, h, to_first) for h in halves]
-    aside = [send(own(h), SIDE, h, to_side) for h in halves]
-    twin = [send(own(h), CORE, h, to_core) for h in halves]
-    second = [send(own(h), SECOND, h, to_second) for h in halves]
-    diag = [send(blocks.at[h, FIRST], DIAG, h, to_side) for h in halves]
-    twin_side = [send(blocks.at[h, SIDE], CORE_SIDE, h, to_core) for h in halves]
-    twin_diag = [send(blocks.at[h, DIAG], CORE_DIAG, h, to_core) for h in halves]
-    plane_first = [send(blocks.at[h, FIRST], CORE_PLANE, h, to_core) for h in halves]
-    plane_second = [send(blocks.at[h, SECOND], CORE_PLANE, h, to_core) for h in halves]
-    mine = [pltpu.make_async_copy(own(h), blocks.at[h, OWN], own_sem.at[h]) for h in halves]
-    for h in halves:
+    pieces = range(PIECES)
+    first = [send(own(h), FIRST, h, to_first) for h in pieces]
+    aside = [send(own(h), SIDE, h, to_side) for h in pieces]
+    twin = [send(own(h), CORE, h, to_core) for h in pieces]
+    second = [send(own(h), SECOND, h, to_second) for h in pieces]
+    diag = [send(blocks.at[h, FIRST], DIAG, h, to_side) for h in pieces]
+    twin_side = [send(blocks.at[h, SIDE], CORE_SIDE, h, to_core) for h in pieces]
+    twin_diag = [send(blocks.at[h, DIAG], CORE_DIAG, h, to_core) for h in pieces]
+    plane_first = [send(blocks.at[h, FIRST], CORE_PLANE, h, to_core) for h in pieces]
+    plane_second = [send(blocks.at[h, SECOND], CORE_PLANE, h, to_core) for h in pieces]
+    mine = [pltpu.make_async_copy(own(h), blocks.at[h, OWN], own_sem.at[h]) for h in pieces]
+    for h in pieces:
         first[h].start()
         aside[h].start()
-    for h in halves:
+    for h in pieces:
         twin[h].start()
         mine[h].start()
 
@@ -126,13 +127,14 @@
                     at = pl.multiple_of(group * (8 * rout) + (low + g) * rout, rout)
                     sketch[pl.ds(at, rout), lanes] = sums[g].astype(jnp.bfloat16)
 
-    for h in halves:
+    for h in pieces:
         first[h].wait_send()
-    for h in halves:
+    for h in pieces[:AHEAD]:
         second[h].start()
-    for h in halves:
+    for h in pieces:
         first[h].wait_recv()
-        diag[h].start()
+        if h < AHEAD:
+            diag[h].start()
 
         @pl.when(side == core)
         def _(h=h):
@@ -144,30 +146,36 @@
     tacc[...] = jnp.zeros_like(tacc)
     qacc[...] = jnp.zeros_like(qacc)
 
-    def score(h, low, high):
-        clusters = []
+    def score(parts, low, high):
+        clusters = {}
         for slot in range(low, high):
             source = lax.rem(b + offsets[slot] + n, n)
             row = qclus_ref[source].astype(jnp.float32)
             full = jnp.transpose(jnp.broadcast_to(row, (tile, tile)))
-            clusters.append(full[h * piece : (h + 1) * piece])
+            for h in parts:
+                clusters[h, slot] = full[h * piece : (h + 1) * piece]
 
         @pl.loop(0, rows // 256)
         def _(step):
             lanes = pl.ds(pl.multiple_of(step * 256, 256), 256)
-            query = blocks[h, low:high].reshape((high - low) * piece, width)
+            query = jnp.concatenate(
+                [blocks[h, low:high].reshape((high - low) * piece, width) for h in parts]
+            )
             dots = jnp.dot(query, sketch[:, lanes], preferred_element_type=jnp.float32)
             for part in range(2):
                 tile_lanes = pl.ds(pl.multiple_of(step * 256 + part * 128, 128), 128)
                 tclus = tclus_ref[:, tile_lanes].astype(jnp.float32)
                 total = tacc[:, tile_lanes]
-                for i, slot in enumerate(range(low, high)):
+                for slot in range(low, high):
                     open_tile = mask_ref[step * 2 + part, offsets[slot] + reach]
                     wanted = jnp.where(open_tile > 0, tclus, -1.0)
-                    got = dots[i * piece : (i + 1) * piece, part * 128 : part * 128 + 128]
-                    got = jnp.where(clusters[i] == wanted, jnp.maximum(got, 0.0), 0.0)
-                    total = total + jnp.sum(got.reshape(piece // 8, 8, 128), axis=0)
-                    qacc[slot, h * piece : (h + 1) * piece, :] += got
+                    for i, h in enumerate(parts):
+                        at = (i * (high - low) + slot - low) * piece
+                        got = dots[at : at + piece, part * 128 : part * 128 + 128]
+                        same = clusters[h, slot] == wanted
+                        got = jnp.where(same, jnp.maximum(got, 0.0), 0.0)
+                        total = total + jnp.sum(got.reshape(piece // 8, 8, 128), axis=0)
+                        qacc[slot, h * piece : (h + 1) * piece, :] += got
                 tacc[:, tile_lanes] = total
 
     def back(slot):
@@ -186,25 +194,31 @@
             if slot != OWN:
                 back(slot).start()
 
-    for h in halves:
-        mine[h].wait()
-        twin[h].wait_recv()
-        twin_side[h].wait_recv()
-        score(h, OWN, SECOND)
+    for parts in (pieces[: PIECES // 2], pieces[PIECES // 2 :]):
+        for h in parts:
+            mine[h].wait()
+            twin[h].wait_recv()
+            twin_side[h].wait_recv()
+        score(parts, OWN, SECOND)
     give_back(OWN, SECOND)
 
-    for h in halves:
+    for h in pieces:
+        diag[h].wait_recv()
+        twin_diag[h].start()
         second[h].wait_recv()
 
         @pl.when(side != core)
         def _(h=h):
             plane_second[h].start()
 
-        diag[h].wait_recv()
-        twin_diag[h].start()
+        if h + AHEAD < PIECES:
+            second[h].wait_send()
+            second[h + AHEAD].start()
+            diag[h].wait_send()
+            diag[h + AHEAD].start()
         twin_diag[h].wait_recv()
         plane_first[h].wait_recv()
-        score(h, SECOND, SLOTS)
+        score((h,), SECOND, SLOTS)
     give_back(SECOND, SLOTS)
 
     train_ref[...] = jnp.sum(tacc[...], axis=0, keepdims=True) * scale
@@ -222,9 +236,12 @@
             total = total + qin[column]
     query_ref[...] = total * scale
 
-    for h in halves:
-        for copy in (aside, twin, second, diag, twin_side, twin_diag, plane_first):
+    for h in pieces:
+        for copy in (aside, twin, twin_side, twin_diag, plane_first):
             copy[h].wait_send()
+    for h in pieces[max(PIECES - AHEAD, 0) :]:
+        second[h].wait_send()
+        diag[h].wait_send()
     for slot in range(1, SLOTS):
         back(slot).wait_send()
 
@@ -237,7 +254,7 @@
     tile, width = queries.shape
     nblocks = lax.axis_size("blk")
     band = pair_mask.shape[1]
-    piece = tile // HALVES
+    piece = tile // PIECES
     vmem = pl.BlockSpec(memory_space=pltpu.VMEM)
     anywhere = pl.BlockSpec(memory_space=pl.ANY)
     train, query = pl.pallas_call(
@@ -257,15 +274,15 @@
             pltpu.VMEM((slots, rin, rows), jnp.float32),
             pltpu.VMEM((slots, rout, rows), jnp.float32),
             pltpu.VMEM((width, rows), jnp.bfloat16),
-            pltpu.VMEM((HALVES, SLOTS, piece, width), jnp.bfloat16),
+            pltpu.VMEM((PIECES, SLOTS, piece, width), jnp.bfloat16),
             pltpu.VMEM((SLOTS, tile, 128), jnp.float32),
             pltpu.VMEM((8, rows), jnp.float32),
             pltpu.VMEM((SLOTS, 1, tile), jnp.float32),
             pltpu.VMEM((band, 1, tile), jnp.float32),
             pltpu.SemaphoreType.DMA((2,)),
-            pltpu.SemaphoreType.DMA((HALVES,)),
-            pltpu.SemaphoreType.DMA((SLOTS, HALVES)),
-            pltpu.SemaphoreType.DMA((SLOTS, HALVES)),
+            pltpu.SemaphoreType.DMA((PIECES,)),
+            pltpu.SemaphoreType.DMA((SLOTS, PIECES)),
+            pltpu.SemaphoreType.DMA((SLOTS, PIECES)),
             pltpu.SemaphoreType.DMA((SLOTS,)),
             pltpu.SemaphoreType.DMA((band,)),
         ],

time: 67.8 us -> 66 us (0.973)
  Pallas kernels: 64.5 us -> 62.7 us
    pallas_call x1, Pallas kernels: 64.5 us -> 62.7 us  [per_device(): pl.pallas_call(kernel, out_shape=(jax.ShapeDtypeStruct((1, rows), jnp.flo...]
where the time goes in v2:
time: 66 us; the launch traced here: 65.8 us
  Pallas kernels  62.7 us (95%)
  local copies, waits for them, and re-layouts  2.4 us (4%)
    pallas_call x1, Pallas kernels, per_device(): pl.pallas_call(kernel, out_shape=(jax.ShapeDtypeStruct((1, rows), jnp.flo...  62.7 us
    unnamed x2, local copies, waits for them, and re-layouts  2.4 us

profile of v2, /device:TPU:0, one launch (start us, length us, event | category | flops | bytes accessed | tf_op | source)
XLA Modules:
  0.0 65.8 jit_solution(16397483985479174745)
XLA Ops:
  0.6 62.7 %score_blocks.1 = (f32[1,1024]{1,0:T(1,128)}, f32[1,128]{1,0:T(1,128)}) custom-call(bf16[16,64,1024]{2,1,0:T(8,128)(2,1)} %bitcast.7, bf16[16,64,1024]{2,1,0:T(8,128)(2,1)} %bitcast.8, s32[1,1024]{1,0:T(1,128)} %bitcast.11, s32[1,1024]{1,0:T(1,128)} %bitcast.12, bf16[128,4096]{1,0:T(8,128)(2,1)} %q_hbm.1, s32[16,1,128]{2,1,0:T(1,128)} %bitcast.9, ...), custom_call_target="tpu_custom_call" | custom-call | tf_op jit(solution)/shard_map/score_blocks/pallas_call | solution.py:260
  63.4 1.3 %copy.11 = f32[1024]{0:T(1024)} copy(f32[1024]{0:T(1024)} %bitcast.10) | data formatting | bytes 8192
  64.6 1.1 %copy.12 = f32[128]{0:T(128)} copy(f32[128]{0:T(128)} %bitcast.13) | data formatting | bytes 1024

commit v3 on v2

--- a/solution.py
+++ b/solution.py
@@ -5,8 +5,8 @@
 from jax.experimental.pallas import tpu as pltpu
 from jax.sharding import PartitionSpec as P
 
-PIECES = 4
-AHEAD = 4
+SHARES = (2, 2, 2, 2)
+PIECES = len(SHARES)
 PLANE = 4
 GROUP = 4
 
@@ -31,7 +31,8 @@
     band = mask_ref.shape[1]
     reach = (band - 1) // 2
     width = rin * rout
-    piece = tile // PIECES
+    sizes = [share * (tile // 8) for share in SHARES]
+    starts = [sum(sizes[:h]) for h in range(PIECES)]
     scale = 1.0 / width**0.5 / 32.0
 
     to_core = b + 1 - 2 * core
@@ -66,12 +67,15 @@
     pl.semaphore_wait(barrier, 2 * reach)
 
     def own(h):
-        return q_hbm.at[pl.ds(h * piece, piece), :]
+        return q_hbm.at[pl.ds(starts[h], sizes[h]), :]
+
+    def held(h, slot):
+        return blocks.at[pl.ds(SLOTS * starts[h] + slot * sizes[h], sizes[h]), :]
 
     def send(src, slot, h, device):
         return pltpu.make_async_remote_copy(
             src_ref=src,
-            dst_ref=blocks.at[h, slot],
+            dst_ref=held(h, slot),
             send_sem=send_sem.at[slot, h],
             recv_sem=recv_sem.at[slot, h],
             device_id={"blk": device},
@@ -83,12 +87,12 @@
     aside = [send(own(h), SIDE, h, to_side) for h in pieces]
     twin = [send(own(h), CORE, h, to_core) for h in pieces]
     second = [send(own(h), SECOND, h, to_second) for h in pieces]
-    diag = [send(blocks.at[h, FIRST], DIAG, h, to_side) for h in pieces]
-    twin_side = [send(blocks.at[h, SIDE], CORE_SIDE, h, to_core) for h in pieces]
-    twin_diag = [send(blocks.at[h, DIAG], CORE_DIAG, h, to_core) for h in pieces]
-    plane_first = [send(blocks.at[h, FIRST], CORE_PLANE, h, to_core) for h in pieces]
-    plane_second = [send(blocks.at[h, SECOND], CORE_PLANE, h, to_core) for h in pieces]
-    mine = [pltpu.make_async_copy(own(h), blocks.at[h, OWN], own_sem.at[h]) for h in pieces]
+    diag = [send(held(h, FIRST), DIAG, h, to_side) for h in pieces]
+    twin_side = [send(held(h, SIDE), CORE_SIDE, h, to_core) for h in pieces]
+    twin_diag = [send(held(h, DIAG), CORE_DIAG, h, to_core) for h in pieces]
+    plane_first = [send(held(h, FIRST), CORE_PLANE, h, to_core) for h in pieces]
+    plane_second = [send(held(h, SECOND), CORE_PLANE, h, to_core) for h in pieces]
+    mine = [pltpu.make_async_copy(own(h), held(h, OWN), own_sem.at[h]) for h in pieces]
     for h in pieces:
         first[h].start()
         aside[h].start()
@@ -129,12 +133,11 @@
 
     for h in pieces:
         first[h].wait_send()
-    for h in pieces[:AHEAD]:
+    for h in pieces:
         second[h].start()
     for h in pieces:
         first[h].wait_recv()
-        if h < AHEAD:
-            diag[h].start()
+        diag[h].start()
 
         @pl.when(side == core)
         def _(h=h):
@@ -153,13 +156,16 @@
             row = qclus_ref[source].astype(jnp.float32)
             full = jnp.transpose(jnp.broadcast_to(row, (tile, tile)))
             for h in parts:
-                clusters[h, slot] = full[h * piece : (h + 1) * piece]
+                clusters[h, slot] = full[starts[h] : starts[h] + sizes[h]]
 
         @pl.loop(0, rows // 256)
         def _(step):
             lanes = pl.ds(pl.multiple_of(step * 256, 256), 256)
             query = jnp.concatenate(
-                [blocks[h, low:high].reshape((high - low) * piece, width) for h in parts]
+                [
+                    blocks[SLOTS * starts[h] + low * sizes[h] : SLOTS * starts[h] + high * sizes[h]]
+                    for h in parts
+                ]
             )
             dots = jnp.dot(query, sketch[:, lanes], preferred_element_type=jnp.float32)
             for part in range(2):
@@ -169,13 +175,14 @@
                 for slot in range(low, high):
                     open_tile = mask_ref[step * 2 + part, offsets[slot] + reach]
                     wanted = jnp.where(open_tile > 0, tclus, -1.0)
-                    for i, h in enumerate(parts):
-                        at = (i * (high - low) + slot - low) * piece
-                        got = dots[at : at + piece, part * 128 : part * 128 + 128]
+                    for h in parts:
+                        before = (starts[h] - starts[parts[0]]) * (high - low)
+                        at = before + (slot - low) * sizes[h]
+                        got = dots[at : at + sizes[h], part * 128 : part * 128 + 128]
                         same = clusters[h, slot] == wanted
                         got = jnp.where(same, jnp.maximum(got, 0.0), 0.0)
-                        total = total + jnp.sum(got.reshape(piece // 8, 8, 128), axis=0)
-                        qacc[slot, h * piece : (h + 1) * piece, :] += got
+                        total = total + jnp.sum(got.reshape(sizes[h] // 8, 8, 128), axis=0)
+                        qacc[slot, starts[h] : starts[h] + sizes[h], :] += got
                 tacc[:, tile_lanes] = total
 
     def back(slot):
@@ -202,23 +209,20 @@
         score(parts, OWN, SECOND)
     give_back(OWN, SECOND)
 
-    for h in pieces:
-        diag[h].wait_recv()
-        twin_diag[h].start()
-        second[h].wait_recv()
-
-        @pl.when(side != core)
-        def _(h=h):
-            plane_second[h].start()
-
-        if h + AHEAD < PIECES:
-            second[h].wait_send()
-            second[h + AHEAD].start()
-            diag[h].wait_send()
-            diag[h + AHEAD].start()
-        twin_diag[h].wait_recv()
-        plane_first[h].wait_recv()
-        score((h,), SECOND, SLOTS)
+    for parts in (pieces[:2], pieces[2:3], pieces[3:]):
+        for h in parts:
+            diag[h].wait_recv()
+            twin_diag[h].start()
+            second[h].wait_recv()
+
+            @pl.when(side != core)
+            def _(h=h):
+                plane_second[h].start()
+
+        for h in parts:
+            twin_diag[h].wait_recv()
+            plane_first[h].wait_recv()
+        score(parts, SECOND, SLOTS)
     give_back(SECOND, SLOTS)
 
     train_ref[...] = jnp.sum(tacc[...], axis=0, keepdims=True) * scale
@@ -237,11 +241,8 @@
     query_ref[...] = total * scale
 
     for h in pieces:
-        for copy in (aside, twin, twin_side, twin_diag, plane_first):
+        for copy in (aside, twin, second, diag, twin_side, twin_diag, plane_first):
             copy[h].wait_send()
-    for h in pieces[max(PIECES - AHEAD, 0) :]:
-        second[h].wait_send()
-        diag[h].wait_send()
     for slot in range(1, SLOTS):
         back(slot).wait_send()
 
@@ -254,7 +255,6 @@
     tile, width = queries.shape
     nblocks = lax.axis_size("blk")
     band = pair_mask.shape[1]
-    piece = tile // PIECES
     vmem = pl.BlockSpec(memory_space=pltpu.VMEM)
     anywhere = pl.BlockSpec(memory_space=pl.ANY)
     train, query = pl.pallas_call(
@@ -274,7 +274,7 @@
             pltpu.VMEM((slots, rin, rows), jnp.float32),
             pltpu.VMEM((slots, rout, rows), jnp.float32),
             pltpu.VMEM((width, rows), jnp.bfloat16),
-            pltpu.VMEM((PIECES, SLOTS, piece, width), jnp.bfloat16),
+            pltpu.VMEM((SLOTS * tile, width), jnp.bfloat16),
             pltpu.VMEM((SLOTS, tile, 128), jnp.float32),
             pltpu.VMEM((8, rows), jnp.float32),
             pltpu.VMEM((SLOTS, 1, tile), jnp.float32),

time: 66 us -> 66 us (level)
  no operation moved by 1% of the time
where the time goes in v3:
time: 66 us; the launch traced here: 65.8 us
  Pallas kernels  62.7 us (95%)
  local copies, waits for them, and re-layouts  2.4 us (4%)
    pallas_call x1, Pallas kernels, per_device(): pl.pallas_call(kernel, out_shape=(jax.ShapeDtypeStruct((1, rows), jnp.flo...  62.7 us
    unnamed x2, local copies, waits for them, and re-layouts  2.4 us

profile of v3, /device:TPU:0, one launch (start us, length us, event | category | flops | bytes accessed | tf_op | source)
XLA Modules:
  0.0 65.8 jit_solution(12867985261598460759)
XLA Ops:
  0.6 62.7 %score_blocks.1 = (f32[1,1024]{1,0:T(1,128)}, f32[1,128]{1,0:T(1,128)}) custom-call(bf16[16,64,1024]{2,1,0:T(8,128)(2,1)} %bitcast.7, bf16[16,64,1024]{2,1,0:T(8,128)(2,1)} %bitcast.8, s32[1,1024]{1,0:T(1,128)} %bitcast.11, s32[1,1024]{1,0:T(1,128)} %bitcast.12, bf16[128,4096]{1,0:T(8,128)(2,1)} %q_hbm.1, s32[16,1,128]{2,1,0:T(1,128)} %bitcast.9, ...), custom_call_target="tpu_custom_call" | custom-call | tf_op jit(solution)/shard_map/score_blocks/pallas_call | solution.py:260
  63.4 1.3 %copy.11 = f32[1024]{0:T(1024)} copy(f32[1024]{0:T(1024)} %bitcast.10) | data formatting | bytes 8192
  64.6 1.1 %copy.12 = f32[128]{0:T(128)} copy(f32[128]{0:T(128)} %bitcast.13) | data formatting | bytes 1024
